TPU v7x, 128 devices: a whole 4x4x4 slice. The times are simulated.
128 devices in a mesh: dp: 8 (over x, core), fsdp: 16 (over y, z).
Axes of the slice: x: 4, y: 4, z: 4, core: 2. Of those that a mesh axis runs over, the one named last changes fastest.
Arguments:
- latents: bfloat16 [256, 512, 512], P(('dp', 'fsdp')), may hold values from -6 to 6
- task_ids: int32 [256], P(('dp', 'fsdp')), may hold values from 0 to 17
- slot_counts: int32 [256], P(('dp', 'fsdp')), may hold values from 128 to 512, as said below
- cotangent: bfloat16 [256, 512, 512], P(('dp', 'fsdp')), may hold values from -6 to 6
- task_embed: bfloat16 [18, 512], P(None, ('dp', 'fsdp')), may hold values from -3 to 3
- norms: bfloat16 [4, 512], P(None, ('dp', 'fsdp')), may hold values from 0.5 to 1.5
- attn_in: bfloat16 [512, 1536], P(('dp', 'fsdp')), may hold values from -0.25 to 0.25
- attn_out: bfloat16 [512, 512], P(('dp', 'fsdp')), may hold values from -2 to 2
- out_biases: bfloat16 [2, 512], P(None, ('dp', 'fsdp')), may hold values from -2 to 2
- mlp_in: bfloat16 [512, 2048], P(('dp', 'fsdp')), may hold values from -0.25 to 0.25
- mlp_in_bias: bfloat16 [2048], P(('dp', 'fsdp')), may hold values from -3 to 3
- mlp_out: bfloat16 [2048, 512], P(('dp', 'fsdp')), may hold values from -0.125 to 0.125
Outputs:
- latents_out: bfloat16 [256, 512, 512], P(('dp', 'fsdp'))
- grad_latents: bfloat16 [256, 512, 512], P(('dp', 'fsdp'))
- grad_task_embed: float32 [18, 512], P(None, ('dp', 'fsdp'))
- grad_norms: float32 [4, 512], P(None, ('dp', 'fsdp'))
- grad_attn_in: float32 [512, 1536], P(('dp', 'fsdp'))
- grad_attn_out: float32 [512, 512], P(('dp', 'fsdp'))
- grad_out_biases: float32 [2, 512], P(None, ('dp', 'fsdp'))
- grad_mlp_in: float32 [512, 2048], P(('dp', 'fsdp'))
- grad_mlp_in_bias: float32 [2048], P(('dp', 'fsdp'))
- grad_mlp_out: float32 [2048, 512], P(('dp', 'fsdp'))
Inputs may be any that keep to these rules, and one draw needn't show every extreme that they name: `slot_counts`: some array has exactly 512 valid slots and some has exactly 128.
All inputs are finite; a program needn't handle non-finite values.
Results may differ from a plain program's by a relative error of at most 0.012.
Values may be sent and summed in bfloat16 or wider, within the bound.
A program may use at most 192 MiB of HBM per device.

v0:
```python
import functools
import math

import jax
import jax.numpy as jnp
from jax import lax
from jax.experimental import pallas as pl
from jax.experimental.pallas import tpu as pltpu
from jax.sharding import PartitionSpec as P

HEADS = 8
EPS = 1e-05
BEST = lax.Precision.HIGHEST
MESH = pl.DeviceIdType.MESH
ALL = slice(None)
ORDERS = (("z", "y", "x"), ("y", "x", "z"), ("x", "z", "y"))
TILES = 12
WAVES = (((0, 1), (1, 1), (2, 1)), ((3, 3), (6, 3), (9, 3)))


def my_position():
    dp, fsdp = lax.axis_index("dp"), lax.axis_index("fsdp")
    return {
        "x": lax.div(dp, 2),
        "c": lax.rem(dp, 2),
        "y": lax.div(fsdp, 4),
        "z": lax.rem(fsdp, 4),
    }


def moved(pos, axis, step):
    size = 2 if axis == "c" else 4
    return {**pos, axis: lax.rem(pos[axis] + step, size)}


def device_of(pos):
    return (pos["x"] * 2 + pos["c"], pos["y"] * 4 + pos["z"])


def greet(pos):
    barrier = pltpu.get_barrier_semaphore()
    partners = [moved(pos, axis, k) for axis in "xyz" for k in (1, 2, 3)] + [moved(pos, "c", 1)]
    for other in partners:
        pl.semaphore_signal(barrier, inc=1, device_id=device_of(other), device_id_type=MESH)
    pl.semaphore_wait(barrier, len(partners))


def remote(src, dst, send, recv, pos):
    return pltpu.make_async_remote_copy(
        src_ref=src, dst_ref=dst, send_sem=send, recv_sem=recv,
        device_id=device_of(pos), device_id_type=MESH,
    )


class Gather:
    def __init__(self, wave, own, tiles, send, recv, pos):
        self.wave, self.own, self.tiles, self.pos = wave, own, tiles, pos
        self.send, self.recv = send, recv

    def slab(self, part, free, at=None):
        first, count = WAVES[self.wave][part]
        place = {**self.pos, **(at or {})}
        index = [ALL if axis in free else place[axis] for axis in "xcyz"]
        return self.tiles.at[(pl.ds(first, count), *index)]

    def stage_copy(self, part, stage, k):
        order = ORDERS[part]
        slab = self.slab(part, order[:stage])
        src = slab
        if stage == 0:
            first, count = WAVES[self.wave][part]
            src = self.own.at[pl.ds(first, count)]
        slot = (self.wave, part, stage * 3 + k - 1)
        return remote(src, slab, self.send.at[slot], self.recv.at[slot], moved(self.pos, order[stage], k))

    def pair_copy(self, part, k):
        order = ORDERS[part]
        at = {order[2]: lax.rem(self.pos[order[2]] + 4 - k, 4)} if k else None
        slab = self.slab(part, order[:2], at)
        slot = (self.wave, part, 9 + k)
        return remote(slab, slab, self.send.at[slot], self.recv.at[slot], moved(self.pos, "c", 1))

    def start(self, stage):
        for part in range(3):
            for k in (2, 1, 3):
                self.stage_copy(part, stage, k).start()
            if stage == 2:
                self.pair_copy(part, 0).start()

    def arrive(self, stage):
        for part in range(3):
            for k in (1, 3, 2):
                self.stage_copy(part, stage, k).wait_recv()
                if stage == 2:
                    self.pair_copy(part, k).start()

    def arrive_pair(self):
        for part in range(3):
            for k in range(4):
                self.pair_copy(part, k).wait_recv()

    def settle(self):
        for part in range(3):
            for stage in range(3):
                for k in (1, 2, 3):
                    self.stage_copy(part, stage, k).wait_send()
            for k in range(4):
                self.pair_copy(part, k).wait_send()


class SmallGather:
    def __init__(self, own, slots, kept, pair, send, recv, pos):
        self.own, self.slots, self.kept, self.pair = own, slots, kept, pair
        self.send, self.recv, self.pos = send, recv, pos

    def copy(self, stage, k):
        here = self.kept.at[self.pos["x"]]
        src = self.own if stage == 0 else here
        dst = here if stage == 2 else self.slots.at[stage, k - 1]
        slot = stage * 3 + k - 1
        return remote(src, dst, self.send.at[slot], self.recv.at[slot], moved(self.pos, "zyx"[stage], k))

    def pair_copy(self):
        return remote(self.kept, self.pair, self.send.at[9], self.recv.at[9], moved(self.pos, "c", 1))

    def start(self, stage):
        for k in (2, 1, 3):
            self.copy(stage, k).start()

    def arrive(self, stage):
        for k in (1, 3, 2):
            self.copy(stage, k).wait_recv()
        if stage == 2:
            self.pair_copy().start()
            return
        total = self.own[...] if stage == 0 else self.kept[self.pos["x"]]
        if stage == 1:
            for k in (1, 2, 3):
                self.copy(1, k).wait_send()
        for k in range(3):
            total = total + self.slots[stage, k]
        self.kept[self.pos["x"]] = total

    def arrive_pair(self, out):
        self.pair_copy().wait_recv()
        for x in range(4):
            out[:, x * 128 : (x + 1) * 128] = self.kept[x].astype(jnp.float32) + self.pair[x].astype(jnp.float32)

    def settle(self):
        for stage in (0, 2):
            for k in (1, 2, 3):
                self.copy(stage, k).wait_send()
        self.pair_copy().wait_send()


class Scatter:
    def __init__(self, wave, tiles, from_pair, from1, from2, from3, send, recv, pos):
        self.wave, self.tiles, self.pos = wave, tiles, pos
        self.from_pair, self.from_stage = from_pair, (from1, from2, from3)
        self.send, self.recv = send, recv

    def order(self, part):
        return ORDERS[part][::-1]

    def span(self, part):
        return WAVES[self.wave][part]

    def pair_copy(self, part):
        first, count = self.span(part)
        other = moved(self.pos, "c", 1)
        slot = (self.wave, part, 9)
        return remote(
            self.tiles.at[pl.ds(first, count), :, other["c"]], self.from_pair.at[pl.ds(first, count)],
            self.send.at[slot], self.recv.at[slot], other,
        )

    def index(self, part, stage, at=None):
        place = {**self.pos, **(at or {})}
        held = self.order(part)[: stage + 1]
        return tuple(place[axis] if axis in held or axis == "c" else ALL for axis in "xcyz")

    def stage_copy(self, part, stage, k):
        first, count = self.span(part)
        axis = self.order(part)[stage]
        other = moved(self.pos, axis, k)
        slot = (self.wave, part, stage * 3 + k - 1)
        src = self.tiles.at[(pl.ds(first, count), *self.index(part, stage, other))]
        dst = self.from_stage[stage].at[pl.ds(first, count), k - 1]
        return remote(src, dst, self.send.at[slot], self.recv.at[slot], other)

    def start_pair(self, part):
        self.pair_copy(part).start()

    def add_pair(self, part):
        first, count = self.span(part)
        self.pair_copy(part).wait_recv()
        core = self.pos["c"]

        def add(i, carry):
            t, x = first + lax.div(i, 4), lax.rem(i, 4)
            total = self.tiles[t, x, core].astype(jnp.float32) + self.from_pair[t, x].astype(jnp.float32)
            self.tiles[t, x, core] = total.astype(jnp.bfloat16)
            return carry

        lax.fori_loop(0, count * 4, add, 0)

    def start(self, part, stage):
        for k in (2, 1, 3):
            self.stage_copy(part, stage, k).start()

    def add(self, part, stage, out=None):
        first, count = self.span(part)
        for k in (1, 3, 2):
            self.stage_copy(part, stage, k).wait_recv()
        index = self.index(part, stage)

        def add(t):
            total = self.tiles[(t, *index)].astype(jnp.float32)
            for k in range(3):
                total = total + self.from_stage[stage][t, k].astype(jnp.float32)
            if stage == 2:
                out[t] = total
            else:
                self.tiles[(t, *index)] = total.astype(jnp.bfloat16)

        for t in range(first, first + count):
            add(t)

    def settle(self):
        for part in range(3):
            self.pair_copy(part).wait_send()
            for stage in range(3):
                for k in (1, 2, 3):
                    self.stage_copy(part, stage, k).wait_send()


class SmallScatter:
    def __init__(self, own, pair, slots, held, send, recv, pos):
        self.own, self.pair, self.slots, self.held = own, pair, slots, held
        self.send, self.recv, self.pos = send, recv, pos

    def pair_copy(self):
        return remote(self.own, self.pair, self.send.at[9], self.recv.at[9], moved(self.pos, "c", 1))

    def copy(self, stage, k):
        other = moved(self.pos, "xyz"[stage], k)
        src = self.held.at[other["x"]] if stage == 0 else self.held.at[3 + stage]
        slot = stage * 3 + k - 1
        return remote(src, self.slots.at[stage, k - 1], self.send.at[slot], self.recv.at[slot], other)

    def add_pair(self):
        self.pair_copy().wait_recv()
        self.held[0:4] = self.own[...] + self.pair[...]

    def start(self, stage):
        for k in (2, 1, 3):
            self.copy(stage, k).start()

    def add(self, stage):
        for k in (1, 3, 2):
            self.copy(stage, k).wait_recv()
        total = self.held[self.pos["x"]] if stage == 0 else self.held[3 + stage]
        for k in range(3):
            total = total + self.slots[stage, k]
        self.held[4 + stage] = total

    def settle(self):
        self.pair_copy().wait_send()
        for stage in range(3):
            for k in (1, 2, 3):
                self.copy(stage, k).wait_send()


def quarter_order(transposed=False):
    a = lax.broadcasted_iota(jnp.int32, (256, 256), 1 if transposed else 0)
    b = lax.broadcasted_iota(jnp.int32, (256, 256), 0 if transposed else 1)
    source = ((a % 64) // 4) * 16 + (a // 64) * 4 + a % 4
    return (source == b).astype(jnp.float32).astype(jnp.bfloat16)


def unfold(tiles, first, count, out):
    order = quarter_order()

    def one(i, carry):
        x, c = lax.div(i, 2), lax.rem(i, 2)
        blocks = [tiles[first + t, x, c].reshape(256, 128) for t in range(count)]
        rows = jnp.dot(order, jnp.concatenate(blocks, 1), preferred_element_type=jnp.float32).astype(jnp.bfloat16)
        for q in range(4):
            out[pl.ds(pl.multiple_of(i * 64, 64), 64), q * count * 128 : (q + 1) * count * 128] = rows[q * 64 : (q + 1) * 64]
        return carry

    lax.fori_loop(0, 8, one, 0)


def unfold_plain(tiles, first, count, out):
    def one(i, carry):
        x, c = lax.div(i, 2), lax.rem(i, 2)
        for t in range(count):
            out[pl.ds(pl.multiple_of(i * 256, 256), 256), t * 128 : (t + 1) * 128] = tiles[first + t, x, c].reshape(256, 128)
        return carry

    lax.fori_loop(0, 8, one, 0)


def fold(grad, tiles, first, count):
    order = quarter_order(True)

    def one(i, carry):
        x, c = lax.div(i, 2), lax.rem(i, 2)
        rows = [
            grad[pl.ds(pl.multiple_of(i * 64, 64), 64), q * count * 128 : (q + 1) * count * 128].astype(jnp.bfloat16)
            for q in range(4)
        ]
        blocks = jnp.dot(order, jnp.concatenate(rows, 0), preferred_element_type=jnp.float32).astype(jnp.bfloat16)
        for t in range(count):
            tiles[first + t, x, c] = blocks[:, t * 128 : (t + 1) * 128].reshape(4, 4, 16, 128)
        return carry

    lax.fori_loop(0, 8, one, 0)


def fold_plain(grad, tiles, first, count):
    def one(i, carry):
        x, c = lax.div(i, 2), lax.rem(i, 2)
        for t in range(count):
            block = grad[pl.ds(pl.multiple_of(i * 256, 256), 256), t * 128 : (t + 1) * 128]
            tiles[first + t, x, c] = block.astype(jnp.bfloat16).reshape(4, 4, 16, 128)
        return carry

    lax.fori_loop(0, 8, one, 0)


def shard_tiles(attn_in, attn_out, mlp_in, mlp_out):
    def quarters(w, count):
        return w.reshape(4, 4, count, 128).transpose(2, 1, 0, 3).reshape(count, 16, 128)

    return jnp.concatenate(
        (
            quarters(attn_in, 3),
            quarters(attn_out, 1),
            quarters(mlp_in, 4),
            mlp_out.reshape(16, 4, 128).transpose(1, 0, 2),
        )
    )


def shard_small(task_embed, norms, out_biases, mlp_in_bias):
    pos = my_position()
    ring = pos["y"] * 4 + pos["z"]
    block = jnp.zeros((32, 128), jnp.bfloat16)
    rows = jnp.concatenate((task_embed, norms, out_biases))
    block = lax.dynamic_update_slice(block, rows, (0, pos["c"] * 64 + ring * 4))
    at = (24 + pos["c"] * 2 + lax.div(ring, 8), 16 * lax.rem(ring, 8))
    return lax.dynamic_update_slice(block, mlp_in_bias[None, :], at)


def own_small(block):
    pos = my_position()
    ring = pos["y"] * 4 + pos["z"]
    columns = lax.dynamic_slice(block, (0, pos["c"] * 64 + ring * 4), (24, 4))
    at = (24 + pos["c"] * 2 + lax.div(ring, 8), 16 * lax.rem(ring, 8))
    bias = lax.dynamic_slice(block, at, (1, 16))[0]
    return columns[0:18], columns[18:22], columns[22:24], bias


def own_weights(total):
    def quarters(t, count):
        return t.reshape(count, 4, 4, 128).transpose(2, 1, 0, 3).reshape(4, 4 * count * 128)

    return quarters(total[0:3], 3), quarters(total[3:4], 1), quarters(total[4:8], 4), total[8:12].transpose(1, 0, 2).reshape(16, 512)


F32, BF16 = jnp.float32, jnp.bfloat16
GELU0 = math.sqrt(2.0 / math.pi)
GELU1 = GELU0 * 0.044715


def nn(a, b):
    return jnp.dot(a, b, preferred_element_type=F32)


def nt(a, b):
    return lax.dot_general(a, b, (((1,), (1,)), ((), ())), preferred_element_type=F32)


def tn(a, b):
    return lax.dot_general(a, b, (((0,), (0,)), ((), ())), preferred_element_type=F32)


def rows_of(i):
    return pl.ds(pl.multiple_of(i * 512, 512), 512)


def normalized(h):
    centred = h - jnp.mean(h, axis=-1, keepdims=True)
    factor = lax.rsqrt(jnp.mean(centred * centred, axis=-1, keepdims=True) + EPS)
    return centred * factor, factor


def normalized_back(grad, unit, factor, gain):
    scaled = grad * gain
    inner = jnp.mean(scaled, axis=-1, keepdims=True)
    along = jnp.mean(scaled * unit, axis=-1, keepdims=True)
    return factor * (scaled - inner - unit * along)


def column_sum(v):
    return jnp.sum(v, axis=0, keepdims=True)


def embedding(r, i):
    row = lax.broadcasted_iota(jnp.int32, (24, 1), 0)
    return column_sum(jnp.where(row == r.task_ids[i], r.params[0:24], 0.0))


def head_lanes(h):
    lane = lax.broadcasted_iota(jnp.int32, (1, 128), 1)
    return ((lane >= 64) == (h == 1)).astype(F32).astype(BF16)


def first_norm(r, i):
    unit, factor = normalized(r.lat[i].astype(F32) + embedding(r, i))
    a1 = (unit * r.params[18:19] + r.params[19:20]).astype(BF16)
    r.a1[rows_of(i)] = a1
    r.u1[rows_of(i)] = unit
    r.r1[rows_of(i)] = factor
    for part in range(3):
        columns = slice(part * 512, (part + 1) * 512)
        result = nn(a1, r.w_qkv[:, columns])
        if part == 0:
            result = result * 0.125
        r.qkv[rows_of(i), columns] = result.astype(BF16)


def pair_of(r, i, hp, part):
    return r.qkv[rows_of(i), pl.ds(pl.multiple_of(part * 512 + hp * 128, 128), 128)]


def attend(r, i, hp):
    q, k, v = (pair_of(r, i, hp, part) for part in range(3))
    slots = lax.broadcasted_iota(jnp.int32, (1, 512), 1)
    bias = jnp.where(slots < r.counts[i], 0.0, -1000000000.0)
    mixed = None
    for h in range(2):
        lanes = head_lanes(h)
        scores = nt(q, k * lanes) + bias
        expo = jnp.exp(scores - jnp.max(scores, axis=-1, keepdims=True)).astype(BF16)
        r.expo[i * 8 + hp * 2 + h] = expo
        wide = jnp.concatenate((v * lanes, jnp.broadcast_to(lanes, (512, 128))), 1)
        term = nn(expo, wide)
        mixed = term if mixed is None else mixed + term
    inverse = 1.0 / mixed[:, 128:]
    columns = pl.ds(pl.multiple_of(hp * 128, 128), 128)
    r.inverse[rows_of(i), columns] = inverse
    mean = mixed[:, :128] * inverse
    r.o32[rows_of(i), columns] = mean
    r.o[rows_of(i), columns] = mean.astype(BF16)


def second_norm(r, i):
    h1 = r.lat[i].astype(F32) + embedding(r, i) + (nn(r.o[rows_of(i)], r.w_out[...]) + r.params[22:23])
    unit, factor = normalized(h1)
    r.a2[rows_of(i)] = (unit * r.params[20:21] + r.params[21:22]).astype(BF16)
    r.u2[rows_of(i)] = unit
    r.r2[rows_of(i)] = factor
    r.result[rows_of(i)] = h1


def feed_forward(r, j):
    units = pl.ds(pl.multiple_of(j * 512, 512), 512)
    tile = pl.ds(pl.multiple_of(j * 128, 128), 128)
    bias = jnp.concatenate([r.params[24 + m : 25 + m, tile] for m in range(4)], 1)
    sums = None
    for i in range(2):
        z = nn(r.a2[rows_of(i)], r.w_up[:, units]) + bias
        z2 = z * z
        half = 0.5 + 0.5 * jnp.tanh(z * (GELU0 + GELU1 * z2))
        act = (z * half).astype(BF16)
        slope = half + z * (2 * GELU0 + 6 * GELU1 * z2) * (half * (1.0 - half))
        gz = (nt(r.y[i], r.w_down[units, :]) * slope).astype(BF16)
        r.act[rows_of(i)] = act
        r.gz[rows_of(i)] = gz
        down = nn(act, r.w_down[units, :])
        back = nt(gz, r.w_up[:, units])
        r.result[rows_of(i)] = r.result[rows_of(i)] + down

        @pl.when(j == 0)
        def _():
            r.back[rows_of(i)] = back

        @pl.when(j > 0)
        def _():
            r.back[rows_of(i)] = r.back[rows_of(i)] + back

        total = column_sum(gz.astype(F32))
        sums = total if sums is None else sums + total
    for m in range(4):
        r.small[j, 24 + m : 25 + m] = sums[:, m * 128 : (m + 1) * 128]
    g_down = tn(r.act[...], r.y[...].reshape(1024, 512)).astype(BF16)
    for c in range(2):
        for t in range(4):
            r.tiles[8 + t, j, c] = g_down[c * 256 : (c + 1) * 256, t * 128 : (t + 1) * 128].reshape(4, 4, 16, 128)
    r.g_up[:, units] = tn(r.a2[...], r.gz[...]).astype(BF16)


def add_small(r, row, value):
    for x in range(4):
        r.small[x, row : row + 1] = r.small[x, row : row + 1] + value[:, x * 128 : (x + 1) * 128]


def second_norm_back(r, i):
    grad, unit = r.back[rows_of(i)], r.u2[rows_of(i)]
    add_small(r, 20, column_sum(grad * unit))
    add_small(r, 21, column_sum(grad))
    y = r.y[i].astype(F32)
    add_small(r, 23, column_sum(y))
    gh1 = y + normalized_back(grad, unit, r.r2[rows_of(i)], r.params[20:21])
    r.back[rows_of(i)] = gh1
    gb = gh1.astype(BF16)
    r.gb[rows_of(i)] = gb
    add_small(r, 22, column_sum(gb.astype(F32)))
    go = (nt(gb, r.w_out[...]) * r.inverse[rows_of(i)]).astype(BF16)
    r.go[rows_of(i)] = go
    product = go.astype(F32) * r.o32[rows_of(i)]
    high = product.astype(BF16).astype(F32)
    low = product - high
    first = lax.broadcasted_iota(jnp.int32, (1, 128), 1) < 64
    for hp in range(4):
        columns = slice(hp * 128, (hp + 1) * 128)
        swapped = pltpu.roll(low[:, columns], 64, 1)
        r.god0[rows_of(i), columns] = jnp.where(first, high[:, columns], swapped).astype(BF16)
        r.god1[rows_of(i), columns] = jnp.where(first, swapped, high[:, columns]).astype(BF16)
    r.out[i] = (r.result[rows_of(i)] + r.params[23:24]).astype(BF16)


def out_gradient(r):
    r.g_out[...] = tn(r.o[...], r.gb[...]).astype(BF16)


def attend_back(r, i, hp):
    q, k, v = (pair_of(r, i, hp, part) for part in range(3))
    columns = pl.ds(pl.multiple_of(hp * 128, 128), 128)
    go = r.go[rows_of(i), columns]
    gq = gk = gv = 0.0
    for h in range(2):
        lanes = head_lanes(h)
        both = jnp.concatenate((go, (r.god0, r.god1)[h][rows_of(i), columns]), 1)
        wide = jnp.concatenate((v * lanes, jnp.full((512, 128), -1.0, BF16)), 1)
        expo = r.expo[i * 8 + hp * 2 + h]
        gs = (expo.astype(F32) * nt(both, wide)).astype(BF16)
        gq = gq + nn(gs, k * lanes)
        gk = gk + tn(gs, q * lanes)
        gv = gv + tn(expo, go * lanes)
    for part, value in enumerate((gq * 0.125, gk, gv)):
        r.qkv[rows_of(i), pl.ds(pl.multiple_of(part * 512 + hp * 128, 128), 128)] = value.astype(BF16)


def first_norm_back(r, i):
    grad, unit = nt(r.qkv[rows_of(i)], r.w_qkv[...]), r.u1[rows_of(i)]
    add_small(r, 18, column_sum(grad * unit))
    add_small(r, 19, column_sum(grad))
    gh0 = r.back[rows_of(i)] + normalized_back(grad, unit, r.r1[rows_of(i)], r.params[18:19])
    r.glat[i] = gh0.astype(BF16)
    total = column_sum(gh0)
    row = lax.broadcasted_iota(jnp.int32, (18, 1), 0)
    for x in range(4):
        mine = jnp.where(row == r.task_ids[i], total[:, x * 128 : (x + 1) * 128], 0.0)
        r.small[x, 0:18] = r.small[x, 0:18] + mine


def in_gradient(r):
    a1 = r.a1[...]
    for part in range(3):
        columns = slice(part * 512, (part + 1) * 512)
        r.g_qkv[:, columns] = tn(a1, r.qkv[:, columns]).astype(BF16)


class Refs:
    def __init__(self, names, refs):
        for name, ref in zip(names, refs, strict=True):
            setattr(self, name, ref)


INPUTS = ("task_ids", "counts", "lat_hbm", "y_hbm", "own", "own_small")
OUTPUTS = ("out_hbm", "glat_hbm", "total", "s_total")
BLOCKS = (TILES, 4, 2, 4, 4, 16, 128)
SCRATCH = {
    "lat": ((2, 512, 512), BF16),
    "y": ((2, 512, 512), BF16),
    "out": ((2, 512, 512), BF16),
    "w_qkv": ((512, 1536), BF16),
    "w_out": ((512, 512), BF16),
    "w_up": ((512, 2048), BF16),
    "w_down": ((2048, 512), BF16),
    "params": ((32, 512), F32),
    "a1": ((1024, 512), BF16),
    "u1": ((1024, 512), F32),
    "r1": ((1024, 1), F32),
    "qkv": ((1024, 1536), BF16),
    "expo": ((16, 512, 512), BF16),
    "o": ((1024, 512), BF16),
    "o32": ((1024, 512), F32),
    "inverse": ((1024, 512), F32),
    "result": ((1024, 512), F32),
    "a2": ((1024, 512), BF16),
    "u2": ((1024, 512), F32),
    "r2": ((1024, 1), F32),
    "act": ((1024, 512), BF16),
    "gz": ((1024, 512), BF16),
    "back": ((1024, 512), F32),
    "gb": ((1024, 512), BF16),
    "g_up": ((512, 2048), BF16),
    "g_qkv": ((512, 1536), BF16),
    "g_out": ((512, 512), BF16),
    "small": ((4, 32, 128), F32),
    "tiles": (BLOCKS, BF16),
    "slots": ((2, 3, 32, 128), BF16),
    "kept": ((4, 32, 128), BF16),
    "pair": ((4, 32, 128), BF16),
    "from_pair": ((TILES, 4, 4, 4, 16, 128), BF16),
    "from1": ((TILES, 3, 4, 4, 16, 128), BF16),
    "from2": ((TILES, 3, 4, 16, 128), BF16),
    "from3": ((TILES, 3, 16, 128), BF16),
    "s_pair": ((4, 32, 128), F32),
    "s_slots": ((3, 3, 32, 128), F32),
    "s_held": ((7, 32, 128), F32),
}
SEMAPHORES = {
    "g_send": (2, 3, 13),
    "g_recv": (2, 3, 13),
    "gs_send": (10,),
    "gs_recv": (10,),
    "r_send": (2, 3, 10),
    "r_recv": (2, 3, 10),
    "rs_send": (10,),
    "rs_recv": (10,),
    "local": (4,),
}


def kernel(*refs):
    r = Refs((*INPUTS, *OUTPUTS, *SCRATCH, *SEMAPHORES), refs)
    r.go, r.god0, r.god1, r.glat = r.act, r.gz, r.a2, r.y
    pos = my_position()
    load_lat = pltpu.make_async_copy(r.lat_hbm, r.lat, r.local.at[0])
    load_y = pltpu.make_async_copy(r.y_hbm, r.y, r.local.at[1])
    store_out = pltpu.make_async_copy(r.out, r.out_hbm, r.local.at[2])
    store_glat = pltpu.make_async_copy(r.glat, r.glat_hbm, r.local.at[3])
    load_lat.start()
    load_y.start()
    greet(pos)
    gathers = [Gather(w, r.own, r.tiles, r.g_send, r.g_recv, pos) for w in range(2)]
    tiny = SmallGather(r.own_small, r.slots, r.kept, r.pair, r.gs_send, r.gs_recv, pos)
    scatters = [
        Scatter(w, r.tiles, r.from_pair, r.from1, r.from2, r.from3, r.r_send, r.r_recv, pos) for w in range(2)
    ]
    tiny_sum = SmallScatter(r.small, r.s_pair, r.s_slots, r.s_held, r.rs_send, r.rs_recv, pos)

    gathers[0].start(0)
    tiny.start(0)
    gathers[1].start(0)
    for t in range(TILES):
        r.tiles[t, pos["x"], pos["c"], pos["y"], pos["z"]] = r.own[t]
    r.small[...] = jnp.zeros_like(r.small)
    for stage in range(3):
        gathers[0].arrive(stage)
        if stage < 2:
            gathers[0].start(stage + 1)
        tiny.arrive(stage)
        if stage < 2:
            tiny.start(stage + 1)
    gathers[1].arrive(0)
    gathers[1].start(1)
    tiny.arrive_pair(r.params)
    gathers[0].arrive_pair()
    unfold(r.tiles, 0, 3, r.w_qkv)
    load_lat.wait()
    lax.fori_loop(0, 2, lambda i, n: (first_norm(r, i), n)[1], 0)
    gathers[1].arrive(1)
    gathers[1].start(2)

    def forward(n, carry):
        attend(r, lax.div(n, 4), lax.rem(n, 4))
        return carry

    lax.fori_loop(0, 4, forward, 0)
    gathers[1].arrive(2)
    lax.fori_loop(4, 8, forward, 0)
    gathers[1].arrive_pair()
    unfold(r.tiles, 3, 1, r.w_out)
    unfold(r.tiles, 4, 4, r.w_up)
    unfold_plain(r.tiles, 8, 4, r.w_down)
    gathers[0].settle()
    gathers[1].settle()
    tiny.settle()
    lax.fori_loop(0, 2, lambda i, n: (second_norm(r, i), n)[1], 0)
    load_y.wait()
    lax.fori_loop(0, 4, lambda j, n: (feed_forward(r, j), n)[1], 0)
    fold(r.g_up, r.tiles, 4, 4)
    for part in (1, 2):
        scatters[1].start_pair(part)
    lax.fori_loop(0, 2, lambda i, n: (second_norm_back(r, i), n)[1], 0)
    store_out.start()
    out_gradient(r)
    fold(r.g_out, r.tiles, 3, 1)
    scatters[1].start_pair(0)
    for part in (1, 2):
        scatters[1].add_pair(part)
        scatters[1].start(part, 0)

    def backward(n, carry):
        attend_back(r, lax.div(n, 4), lax.rem(n, 4))

        @pl.when(n == 0)
        def _():
            scatters[1].add_pair(0)
            scatters[1].start(0, 0)

        @pl.when(n == 4)
        def _():
            for part in (1, 2, 0):
                scatters[1].add(part, 0)
                scatters[1].start(part, 1)

        @pl.when(n == 6)
        def _():
            for part in (1, 2, 0):
                scatters[1].add(part, 1)
                scatters[1].start(part, 2)

        return carry

    lax.fori_loop(0, 8, backward, 0)
    in_gradient(r)
    fold(r.g_qkv, r.tiles, 0, 3)
    for part in range(3):
        scatters[0].start_pair(part)
    for part in range(3):
        scatters[1].add(part, 2, r.total)
    lax.fori_loop(0, 2, lambda i, n: (first_norm_back(r, i), n)[1], 0)
    tiny_sum.pair_copy().start()
    store_glat.start()
    for part in range(3):
        scatters[0].add_pair(part)
        scatters[0].start(part, 0)
    tiny_sum.add_pair()
    tiny_sum.start(0)
    for stage in range(3):
        for part in range(3):
            scatters[0].add(part, stage, r.total)
            if stage < 2:
                scatters[0].start(part, stage + 1)
        tiny_sum.add(stage)
        if stage < 2:
            tiny_sum.start(stage + 1)
    r.s_total[...] = r.s_held[6]
    scatters[0].settle()
    scatters[1].settle()
    tiny_sum.settle()
    store_out.wait()
    store_glat.wait()


def whole(task_ids, counts, latents, cotangent, own, small):
    vmem = pl.BlockSpec(memory_space=pltpu.VMEM)
    smem = pl.BlockSpec(memory_space=pltpu.SMEM)
    hbm = pl.BlockSpec(memory_space=pl.ANY)
    array = jax.ShapeDtypeStruct(latents.shape, BF16)
    return pl.pallas_call(
        kernel,
        out_shape=[
            array,
            array,
            jax.ShapeDtypeStruct((TILES, 16, 128), F32),
            jax.ShapeDtypeStruct((32, 128), F32),
        ],
        in_specs=[smem, smem, hbm, hbm, vmem, vmem],
        out_specs=[hbm, hbm, vmem, vmem],
        scratch_shapes=[pltpu.VMEM(shape, dtype) for shape, dtype in SCRATCH.values()]
        + [pltpu.SemaphoreType.DMA(shape) for shape in SEMAPHORES.values()],
        compiler_params=pltpu.CompilerParams(
            collective_id=0, has_side_effects=True, vmem_limit_bytes=60 * 2**20
        ),
    )(task_ids, counts, latents, cotangent, own, small)


def body(
    latents,
    task_ids,
    slot_counts,
    cotangent,
    task_embed,
    norms,
    attn_in,
    attn_out,
    out_biases,
    mlp_in,
    mlp_in_bias,
    mlp_out,
):
    own = shard_tiles(attn_in, attn_out, mlp_in, mlp_out)
    small = shard_small(task_embed, norms, out_biases, mlp_in_bias)
    result, grad_lat, total, s_total = whole(task_ids, slot_counts, latents, cotangent, own, small)
    s_qkv, s_out, s_up, s_down = own_weights(total)
    s_table, s_norms, s_biases, s_bias = own_small(s_total)
    return (result, grad_lat, s_table, s_norms, s_qkv, s_out, s_biases, s_up, s_bias, s_down)


def solution(mesh):
    in_specs = (
        P(("dp", "fsdp"), None, None),
        P(("dp", "fsdp")),
        P(("dp", "fsdp")),
        P(("dp", "fsdp"), None, None),
        P(None, ("dp", "fsdp")),
        P(None, ("dp", "fsdp")),
        P(("dp", "fsdp"), None),
        P(("dp", "fsdp"), None),
        P(None, ("dp", "fsdp")),
        P(("dp", "fsdp"), None),
        P(("dp", "fsdp")),
        P(("dp", "fsdp"), None),
    )
    out_specs = (
        P(("dp", "fsdp"), None, None),
        P(("dp", "fsdp"), None, None),
        P(None, ("dp", "fsdp")),
        P(None, ("dp", "fsdp")),
        P(("dp", "fsdp"), None),
        P(("dp", "fsdp"), None),
        P(None, ("dp", "fsdp")),
        P(("dp", "fsdp"), None),
        P(("dp", "fsdp")),
        P(("dp", "fsdp"), None),
    )
    return jax.shard_map(body, mesh=mesh, in_specs=in_specs, out_specs=out_specs, check_vma=False)
```

profile of v0, /device:TPU:0, one launch (start us, length us, event | category | flops | bytes accessed | tf_op | source)
XLA Modules:
  0.0 134.8 jit_solution(7178792766994979198)
XLA Ops:
  0.6 0.0 copy-start
  0.7 0.0 copy-start.6
  0.7 0.7 copy-done.6
  1.4 0.0 copy-start.7
  1.4 0.0 copy-start.8
  1.4 0.1 copy.56
  1.5 0.6 copy-done.7
  2.0 0.0 copy-done.8
  2.1 0.0 copy-start.3
  2.1 0.4 dynamic_update_slice.6
  2.5 0.0 copy-start.9
  2.5 0.6 copy-done.9
  3.2 0.1 dynamic_update_slice.7.refs_5_
  3.3 0.0 copy-done.3
  3.3 0.0 copy-start.2
  3.3 0.6 copy-done.2
  3.9 0.0 copy-start.4
  3.9 0.7 copy-done.4
  4.6 0.0 copy-done
  4.6 0.0 copy-start.5
  4.7 0.7 copy-done.5
  5.3 0.6 pad_maximum_fusion.refs_4_
  5.9 115.4 %shard_map.195 = (bf16[2,512,512]{2,1,0:T(8,128)(2,1)}, bf16[2,512,512]{2,1,0:T(8,128)(2,1)}, f32[12,16,128]{2,1,0:T(8,128)}, f32[32,128]{1,0:T(8,128)}) custom-call(s32[2]{0:T(128)} %refs_0_.1, s32[2]{0:T(128)} %refs_1_.1, bf16[2,512,512]{2,1,0:T(8,128)(2,1)} %refs_2_.1, bf16[2,512,512]{2,1,0:T(8,128)(2,1)} %refs_3_.1, ...), custom_call_target="tpu_custom_call" | custom-call | tf_op jit(solution)/shard_map/pallas_call | solution.py:769
  121.4 1.3 dynamic-slice_bitcast_fusion
  122.6 0.8 constant_dynamic-slice_fusion
  123.4 0.7 copy.61
  124.1 1.3 dynamic-slice.1
  125.4 1.3 dynamic-slice.2
  126.7 0.8 slice_bitcast_fusion
  127.5 0.6 reshape.74
  128.1 0.6 copy.67
  128.8 0.7 slice.23
  129.5 0.6 reshape.70
  130.1 1.3 slice.24
  131.4 0.0 copy-start.1
  131.4 2.4 %copy.73 = bf16[2,512,512]{2,1,0:T(8,128)(2,1)} copy(bf16[2,512,512]{2,1,0:T(8,128)(2,1)} %get-tuple-element.70) | data formatting | bytes 2097152
  133.8 0.0 copy-done.1
  133.8 1.0 copy.74
  (9 shorter events, 0.1 us)
Async XLA Ops:
  0.6 4.0 %copy-start = (bf16[16,512]{1,0:T(8,128)(2,1)S(1)}, bf16[16,512]{1,0:T(8,128)(2,1)}, u32[]{:S(2)}) copy-start(bf16[16,512]{1,0:T(8,128)(2,1)} %param.23) | copy-start | bytes 49156
  0.7 0.7 copy-start.6
  1.4 0.7 copy-start.7
  1.4 0.7 copy-start.8
  2.1 1.2 copy-start.3
  2.5 0.7 copy-start.9
  3.3 0.6 copy-start.2
  3.9 0.7 copy-start.4
  4.6 0.7 copy-start.5
  131.4 2.4 %copy-start.1 = (bf16[2,512,512]{2,1,0:T(8,128)(2,1)S(1)}, bf16[2,512,512]{2,1,0:T(8,128)(2,1)}, u32[]{:S(2)}) copy-start(bf16[2,512,512]{2,1,0:T(8,128)(2,1)} %get-tuple-element.71) | copy-start | bytes 3145732
where the time goes:
time: 135 us
  Pallas kernels  115 us (85%)
  local copies, waits for them, and re-layouts  17.9 us (13%)
    pallas_call x1, Pallas kernels, whole(): pl.pallas_call(kernel, out_shape=[array, array, jax.ShapeDtypeStruct((TIL...  115 us
    unnamed x25, local copies, waits for them, and re-layouts  8.72 us
    slice x3, local copies, waits for them, and re-layouts, own_small(): return (columns[0:18], columns[18:22], columns[22:24], bias)  3.39 us

commit v1 on v0

--- a/solution.py
+++ b/solution.py
@@ -37,12 +37,18 @@
     return (pos["x"] * 2 + pos["c"], pos["y"] * 4 + pos["z"])
 
 
+def partners_of(pos):
+    return [moved(pos, axis, k) for axis in "xyz" for k in (1, 2, 3)] + [moved(pos, "c", 1)]
+
+
 def greet(pos):
     barrier = pltpu.get_barrier_semaphore()
-    partners = [moved(pos, axis, k) for axis in "xyz" for k in (1, 2, 3)] + [moved(pos, "c", 1)]
-    for other in partners:
+    for other in partners_of(pos):
         pl.semaphore_signal(barrier, inc=1, device_id=device_of(other), device_id_type=MESH)
-    pl.semaphore_wait(barrier, len(partners))
+
+
+def greeted(pos):
+    pl.semaphore_wait(pltpu.get_barrier_semaphore(), 10)
 
 
 def remote(src, dst, send, recv, pos):
@@ -94,10 +100,9 @@
                 if stage == 2:
                     self.pair_copy(part, k).start()
 
-    def arrive_pair(self):
-        for part in range(3):
-            for k in range(4):
-                self.pair_copy(part, k).wait_recv()
+    def arrive_pair(self, part):
+        for k in range(4):
+            self.pair_copy(part, k).wait_recv()
 
     def settle(self):
         for part in range(3):
@@ -154,9 +159,9 @@
 
 
 class Scatter:
-    def __init__(self, wave, tiles, from_pair, from1, from2, from3, send, recv, pos):
+    def __init__(self, wave, tiles, from1, from2, from3, send, recv, pos):
         self.wave, self.tiles, self.pos = wave, tiles, pos
-        self.from_pair, self.from_stage = from_pair, (from1, from2, from3)
+        self.from_stage = (from1, from2, from3)
         self.send, self.recv = send, recv
 
     def order(self, part):
@@ -164,15 +169,6 @@
 
     def span(self, part):
         return WAVES[self.wave][part]
-
-    def pair_copy(self, part):
-        first, count = self.span(part)
-        other = moved(self.pos, "c", 1)
-        slot = (self.wave, part, 9)
-        return remote(
-            self.tiles.at[pl.ds(first, count), :, other["c"]], self.from_pair.at[pl.ds(first, count)],
-            self.send.at[slot], self.recv.at[slot], other,
-        )
 
     def index(self, part, stage, at=None):
         place = {**self.pos, **(at or {})}
@@ -188,22 +184,6 @@
         dst = self.from_stage[stage].at[pl.ds(first, count), k - 1]
         return remote(src, dst, self.send.at[slot], self.recv.at[slot], other)
 
-    def start_pair(self, part):
-        self.pair_copy(part).start()
-
-    def add_pair(self, part):
-        first, count = self.span(part)
-        self.pair_copy(part).wait_recv()
-        core = self.pos["c"]
-
-        def add(i, carry):
-            t, x = first + lax.div(i, 4), lax.rem(i, 4)
-            total = self.tiles[t, x, core].astype(jnp.float32) + self.from_pair[t, x].astype(jnp.float32)
-            self.tiles[t, x, core] = total.astype(jnp.bfloat16)
-            return carry
-
-        lax.fori_loop(0, count * 4, add, 0)
-
     def start(self, part, stage):
         for k in (2, 1, 3):
             self.stage_copy(part, stage, k).start()
@@ -228,10 +208,46 @@
 
     def settle(self):
         for part in range(3):
-            self.pair_copy(part).wait_send()
             for stage in range(3):
                 for k in (1, 2, 3):
                     self.stage_copy(part, stage, k).wait_send()
+
+
+class PairSum:
+    def __init__(self, tiles, from_pair, send, recv, pos):
+        self.tiles, self.from_pair, self.send, self.recv, self.pos = tiles, from_pair, send, recv, pos
+
+    def tile(self, t):
+        other = moved(self.pos, "c", 1)
+        return remote(self.tiles.at[t, :, other["c"]], self.from_pair.at[t], self.send.at[t], self.recv.at[t], other)
+
+    def down(self, j):
+        other = moved(self.pos, "c", 1)
+        return remote(
+            self.tiles.at[pl.ds(8, 4), j, other["c"]], self.from_pair.at[pl.ds(8, 4), j],
+            self.send.at[8 + j], self.recv.at[8 + j], other,
+        )
+
+    def add(self, t, x):
+        core = self.pos["c"]
+        total = self.tiles[t, x, core].astype(jnp.float32) + self.from_pair[t, x].astype(jnp.float32)
+        self.tiles[t, x, core] = total.astype(jnp.bfloat16)
+
+    def add_tile(self, t):
+        self.tile(t).wait_recv()
+        for x in range(4):
+            self.add(t, x)
+
+    def add_down(self, j):
+        self.down(j).wait_recv()
+        for t in range(8, 12):
+            self.add(t, j)
+
+    def settle(self):
+        for t in range(8):
+            self.tile(t).wait_send()
+        for j in range(4):
+            self.down(j).wait_send()
 
 
 class SmallScatter:
@@ -271,6 +287,15 @@
                 self.copy(stage, k).wait_send()
 
 
+COLUMNS = (
+    (0, 4, 8, 1),
+    (5, 9, 2, 6),
+    (10, 3, 7, 11),
+    (0, 1, 2, 3),
+    *(tuple(range(4 * j, 4 * j + 4)) for j in range(4)),
+)
+
+
 def quarter_order(transposed=False):
     a = lax.broadcasted_iota(jnp.int32, (256, 256), 1 if transposed else 0)
     b = lax.broadcasted_iota(jnp.int32, (256, 256), 0 if transposed else 1)
@@ -278,96 +303,33 @@
     return (source == b).astype(jnp.float32).astype(jnp.bfloat16)
 
 
-def unfold(tiles, first, count, out):
-    order = quarter_order()
-
-    def one(i, carry):
+def unfold(r, t, out):
+    blocks = [r.tiles[t, xc // 2, xc % 2].reshape(256, 128) for xc in range(8)]
+    rows = nn(quarter_order(), jnp.concatenate(blocks, 1)).astype(jnp.bfloat16)
+    for q, ct in enumerate(COLUMNS[t]):
+        for xc in range(8):
+            out[xc * 64 : (xc + 1) * 64, ct * 128 : (ct + 1) * 128] = rows[q * 64 : (q + 1) * 64, xc * 128 : (xc + 1) * 128]
+
+
+def unfold_plain(r, out):
+    def one(i):
         x, c = lax.div(i, 2), lax.rem(i, 2)
-        blocks = [tiles[first + t, x, c].reshape(256, 128) for t in range(count)]
-        rows = jnp.dot(order, jnp.concatenate(blocks, 1), preferred_element_type=jnp.float32).astype(jnp.bfloat16)
-        for q in range(4):
-            out[pl.ds(pl.multiple_of(i * 64, 64), 64), q * count * 128 : (q + 1) * count * 128] = rows[q * 64 : (q + 1) * 64]
-        return carry
-
-    lax.fori_loop(0, 8, one, 0)
-
-
-def unfold_plain(tiles, first, count, out):
-    def one(i, carry):
-        x, c = lax.div(i, 2), lax.rem(i, 2)
-        for t in range(count):
-            out[pl.ds(pl.multiple_of(i * 256, 256), 256), t * 128 : (t + 1) * 128] = tiles[first + t, x, c].reshape(256, 128)
-        return carry
-
-    lax.fori_loop(0, 8, one, 0)
-
-
-def fold(grad, tiles, first, count):
-    order = quarter_order(True)
-
-    def one(i, carry):
-        x, c = lax.div(i, 2), lax.rem(i, 2)
-        rows = [
-            grad[pl.ds(pl.multiple_of(i * 64, 64), 64), q * count * 128 : (q + 1) * count * 128].astype(jnp.bfloat16)
-            for q in range(4)
-        ]
-        blocks = jnp.dot(order, jnp.concatenate(rows, 0), preferred_element_type=jnp.float32).astype(jnp.bfloat16)
-        for t in range(count):
-            tiles[first + t, x, c] = blocks[:, t * 128 : (t + 1) * 128].reshape(4, 4, 16, 128)
-        return carry
-
-    lax.fori_loop(0, 8, one, 0)
-
-
-def fold_plain(grad, tiles, first, count):
-    def one(i, carry):
-        x, c = lax.div(i, 2), lax.rem(i, 2)
-        for t in range(count):
-            block = grad[pl.ds(pl.multiple_of(i * 256, 256), 256), t * 128 : (t + 1) * 128]
-            tiles[first + t, x, c] = block.astype(jnp.bfloat16).reshape(4, 4, 16, 128)
-        return carry
-
-    lax.fori_loop(0, 8, one, 0)
-
-
-def shard_tiles(attn_in, attn_out, mlp_in, mlp_out):
-    def quarters(w, count):
-        return w.reshape(4, 4, count, 128).transpose(2, 1, 0, 3).reshape(count, 16, 128)
-
-    return jnp.concatenate(
-        (
-            quarters(attn_in, 3),
-            quarters(attn_out, 1),
-            quarters(mlp_in, 4),
-            mlp_out.reshape(16, 4, 128).transpose(1, 0, 2),
-        )
-    )
-
-
-def shard_small(task_embed, norms, out_biases, mlp_in_bias):
-    pos = my_position()
+        for t in range(4):
+            out[pl.ds(pl.multiple_of(i * 256, 256), 256), t * 128 : (t + 1) * 128] = r.tiles[8 + t, x, c].reshape(256, 128)
+
+    loop(8, one)
+
+
+def fold(r, columns, t):
+    rows = [jnp.concatenate([block[xc * 64 : (xc + 1) * 64] for xc in range(8)], 1) for block in columns]
+    blocks = nn(quarter_order(True), jnp.concatenate(rows, 0)).astype(jnp.bfloat16)
+    for xc in range(8):
+        r.tiles[t, xc // 2, xc % 2] = blocks[:, xc * 128 : (xc + 1) * 128].reshape(4, 4, 16, 128)
+
+
+def small_place(pos):
     ring = pos["y"] * 4 + pos["z"]
-    block = jnp.zeros((32, 128), jnp.bfloat16)
-    rows = jnp.concatenate((task_embed, norms, out_biases))
-    block = lax.dynamic_update_slice(block, rows, (0, pos["c"] * 64 + ring * 4))
-    at = (24 + pos["c"] * 2 + lax.div(ring, 8), 16 * lax.rem(ring, 8))
-    return lax.dynamic_update_slice(block, mlp_in_bias[None, :], at)
-
-
-def own_small(block):
-    pos = my_position()
-    ring = pos["y"] * 4 + pos["z"]
-    columns = lax.dynamic_slice(block, (0, pos["c"] * 64 + ring * 4), (24, 4))
-    at = (24 + pos["c"] * 2 + lax.div(ring, 8), 16 * lax.rem(ring, 8))
-    bias = lax.dynamic_slice(block, at, (1, 16))[0]
-    return columns[0:18], columns[18:22], columns[22:24], bias
-
-
-def own_weights(total):
-    def quarters(t, count):
-        return t.reshape(count, 4, 4, 128).transpose(2, 1, 0, 3).reshape(4, 4 * count * 128)
-
-    return quarters(total[0:3], 3), quarters(total[3:4], 1), quarters(total[4:8], 4), total[8:12].transpose(1, 0, 2).reshape(16, 512)
+    return pos["c"] * 64 + ring * 4, 24 + pos["c"] * 2 + lax.div(ring, 8), 16 * lax.rem(ring, 8)
 
 
 F32, BF16 = jnp.float32, jnp.bfloat16
@@ -478,11 +440,9 @@
         act = (z * half).astype(BF16)
         slope = half + z * (2 * GELU0 + 6 * GELU1 * z2) * (half * (1.0 - half))
         gz = (nt(r.y[i], r.w_down[units, :]) * slope).astype(BF16)
-        r.act[rows_of(i)] = act
+        r.act[rows_of(i), units] = act
         r.gz[rows_of(i)] = gz
-        down = nn(act, r.w_down[units, :])
         back = nt(gz, r.w_up[:, units])
-        r.result[rows_of(i)] = r.result[rows_of(i)] + down
 
         @pl.when(j == 0)
         def _():
@@ -496,11 +456,12 @@
         sums = total if sums is None else sums + total
     for m in range(4):
         r.small[j, 24 + m : 25 + m] = sums[:, m * 128 : (m + 1) * 128]
-    g_down = tn(r.act[...], r.y[...].reshape(1024, 512)).astype(BF16)
+    g_down = tn(r.act[:, units], r.y[...].reshape(1024, 512)).astype(BF16)
     for c in range(2):
         for t in range(4):
             r.tiles[8 + t, j, c] = g_down[c * 256 : (c + 1) * 256, t * 128 : (t + 1) * 128].reshape(4, 4, 16, 128)
-    r.g_up[:, units] = tn(r.a2[...], r.gz[...]).astype(BF16)
+    g_up = tn(r.a2[...], r.gz[...]).astype(BF16)
+    fold(r, [g_up[:, q * 128 : (q + 1) * 128] for q in range(4)], 4 + j)
 
 
 def add_small(r, row, value):
@@ -530,11 +491,15 @@
         swapped = pltpu.roll(low[:, columns], 64, 1)
         r.god0[rows_of(i), columns] = jnp.where(first, high[:, columns], swapped).astype(BF16)
         r.god1[rows_of(i), columns] = jnp.where(first, swapped, high[:, columns]).astype(BF16)
-    r.out[i] = (r.result[rows_of(i)] + r.params[23:24]).astype(BF16)
 
 
 def out_gradient(r):
-    r.g_out[...] = tn(r.o[...], r.gb[...]).astype(BF16)
+    g_out = tn(r.o[...], r.gb[...]).astype(BF16)
+    fold(r, [g_out[:, q * 128 : (q + 1) * 128] for q in range(4)], 3)
+
+
+def result_of(r, i):
+    r.out[i] = (r.result[rows_of(i)] + nn(r.act[rows_of(i)], r.w_down[...]) + r.params[23:24]).astype(BF16)
 
 
 def attend_back(r, i, hp):
@@ -568,11 +533,10 @@
         r.small[x, 0:18] = r.small[x, 0:18] + mine
 
 
-def in_gradient(r):
-    a1 = r.a1[...]
-    for part in range(3):
-        columns = slice(part * 512, (part + 1) * 512)
-        r.g_qkv[:, columns] = tn(a1, r.qkv[:, columns]).astype(BF16)
+def in_gradient(r, t):
+    columns = jnp.concatenate([r.qkv[:, ct * 128 : (ct + 1) * 128] for ct in COLUMNS[t]], 1)
+    g_in = tn(r.a1[...], columns).astype(BF16)
+    fold(r, [g_in[:, q * 128 : (q + 1) * 128] for q in range(4)], t)
 
 
 class Refs:
@@ -581,10 +545,25 @@
             setattr(self, name, ref)
 
 
-INPUTS = ("task_ids", "counts", "lat_hbm", "y_hbm", "own", "own_small")
+RAW = {
+    "raw_in": ((4, 1536), BF16),
+    "raw_out": ((4, 512), BF16),
+    "raw_up": ((4, 2048), BF16),
+    "raw_down": ((16, 512), BF16),
+    "raw_table": ((18, 4), BF16),
+    "raw_norms": ((4, 4), BF16),
+    "raw_biases": ((2, 4), BF16),
+    "raw_up_bias": ((1, 16), BF16),
+}
+INPUTS = ("task_ids", "counts", "lat_hbm", "y_hbm", *(f"{name}_hbm" for name in RAW))
 OUTPUTS = ("out_hbm", "glat_hbm", "total", "s_total")
 BLOCKS = (TILES, 4, 2, 4, 4, 16, 128)
 SCRATCH = {
+    **RAW,
+    "own32": ((TILES, 16, 128), F32),
+    "own": ((TILES, 16, 128), BF16),
+    "small32": ((40, 128), F32),
+    "own_small": ((32, 128), BF16),
     "lat": ((2, 512, 512), BF16),
     "y": ((2, 512, 512), BF16),
     "out": ((2, 512, 512), BF16),
@@ -605,13 +584,11 @@
     "a2": ((1024, 512), BF16),
     "u2": ((1024, 512), F32),
     "r2": ((1024, 1), F32),
-    "act": ((1024, 512), BF16),
+    "act": ((1024, 2048), BF16),
     "gz": ((1024, 512), BF16),
+    "god0": ((1024, 512), BF16),
     "back": ((1024, 512), F32),
     "gb": ((1024, 512), BF16),
-    "g_up": ((512, 2048), BF16),
-    "g_qkv": ((512, 1536), BF16),
-    "g_out": ((512, 512), BF16),
     "small": ((4, 32, 128), F32),
     "tiles": (BLOCKS, BF16),
     "slots": ((2, 3, 32, 128), BF16),
@@ -630,35 +607,70 @@
     "g_recv": (2, 3, 13),
     "gs_send": (10,),
     "gs_recv": (10,),
-    "r_send": (2, 3, 10),
-    "r_recv": (2, 3, 10),
+    "p_send": (12,),
+    "p_recv": (12,),
+    "r_send": (2, 3, 9),
+    "r_recv": (2, 3, 9),
     "rs_send": (10,),
     "rs_recv": (10,),
-    "local": (4,),
+    "local": (12,),
 }
+
+
+def alias(r):
+    r.go, r.god1, r.glat = r.gz, r.a2, r.y
+
+
+def loop(count, step):
+    lax.fori_loop(0, count, lambda n, carry: (step(n), carry)[1], 0)
+
+
+def pack_own(r, pos):
+    for t, blocks in enumerate(COLUMNS):
+        raw = (r.raw_in, r.raw_out, r.raw_up)[0 if t < 3 else 1 if t == 3 else 2]
+        for q, ct in enumerate(blocks):
+            r.own32[t, 4 * q : 4 * q + 4] = raw[:, ct * 128 : (ct + 1) * 128].astype(F32)
+    for t in range(8):
+        r.own[t] = r.own32[t].astype(BF16)
+    for t in range(4):
+        r.own[8 + t] = r.raw_down[:, t * 128 : (t + 1) * 128]
+    r.small32[...] = jnp.zeros_like(r.small32)
+    r.small32[0:18, 0:4] = r.raw_table[...].astype(F32)
+    r.small32[18:22, 0:4] = r.raw_norms[...].astype(F32)
+    r.small32[22:24, 0:4] = r.raw_biases[...].astype(F32)
+    r.small32[32:33, 0:16] = r.raw_up_bias[...].astype(F32)
+    offset, bias_row, bias_offset = small_place(pos)
+    block = pltpu.roll(r.small32[0:32], offset, 1)
+    bias = pltpu.roll(r.small32[32:40], bias_offset, 1)[0:1]
+    row = lax.broadcasted_iota(jnp.int32, (32, 1), 0)
+    r.own_small[...] = (block + jnp.where(row == bias_row, bias, 0.0)).astype(BF16)
 
 
 def kernel(*refs):
     r = Refs((*INPUTS, *OUTPUTS, *SCRATCH, *SEMAPHORES), refs)
-    r.go, r.god0, r.god1, r.glat = r.act, r.gz, r.a2, r.y
+    alias(r)
     pos = my_position()
-    load_lat = pltpu.make_async_copy(r.lat_hbm, r.lat, r.local.at[0])
-    load_y = pltpu.make_async_copy(r.y_hbm, r.y, r.local.at[1])
-    store_out = pltpu.make_async_copy(r.out, r.out_hbm, r.local.at[2])
-    store_glat = pltpu.make_async_copy(r.glat, r.glat_hbm, r.local.at[3])
-    load_lat.start()
-    load_y.start()
+    loads = [
+        pltpu.make_async_copy(getattr(r, f"{name}_hbm"), getattr(r, name), r.local.at[n])
+        for n, name in enumerate((*RAW, "lat", "y"))
+    ]
+    store_out = pltpu.make_async_copy(r.out, r.out_hbm, r.local.at[10])
+    store_glat = pltpu.make_async_copy(r.glat, r.glat_hbm, r.local.at[11])
     greet(pos)
+    for load in loads:
+        load.start()
     gathers = [Gather(w, r.own, r.tiles, r.g_send, r.g_recv, pos) for w in range(2)]
     tiny = SmallGather(r.own_small, r.slots, r.kept, r.pair, r.gs_send, r.gs_recv, pos)
-    scatters = [
-        Scatter(w, r.tiles, r.from_pair, r.from1, r.from2, r.from3, r.r_send, r.r_recv, pos) for w in range(2)
-    ]
+    pairs = PairSum(r.tiles, r.from_pair, r.p_send, r.p_recv, pos)
+    scatters = [Scatter(w, r.tiles, r.from1, r.from2, r.from3, r.r_send, r.r_recv, pos) for w in range(2)]
     tiny_sum = SmallScatter(r.small, r.s_pair, r.s_slots, r.s_held, r.rs_send, r.rs_recv, pos)
+    for load in loads[:8]:
+        load.wait()
+    pack_own(r, pos)
+    greeted(pos)
 
     gathers[0].start(0)
     tiny.start(0)
-    gathers[1].start(0)
     for t in range(TILES):
         r.tiles[t, pos["x"], pos["c"], pos["y"], pos["z"]] = r.own[t]
     r.small[...] = jnp.zeros_like(r.small)
@@ -669,104 +681,182 @@
         tiny.arrive(stage)
         if stage < 2:
             tiny.start(stage + 1)
+        if stage == 0:
+            gathers[1].start(0)
     gathers[1].arrive(0)
     gathers[1].start(1)
     tiny.arrive_pair(r.params)
-    gathers[0].arrive_pair()
-    unfold(r.tiles, 0, 3, r.w_qkv)
-    load_lat.wait()
-    lax.fori_loop(0, 2, lambda i, n: (first_norm(r, i), n)[1], 0)
+    for t in range(3):
+        gathers[0].arrive_pair(t)
+        unfold(r, t, r.w_qkv)
+    loads[8].wait()
+    loop(2, lambda i: first_norm(r, i))
     gathers[1].arrive(1)
     gathers[1].start(2)
 
-    def forward(n, carry):
+    def forward(n):
         attend(r, lax.div(n, 4), lax.rem(n, 4))
-        return carry
-
-    lax.fori_loop(0, 4, forward, 0)
-    gathers[1].arrive(2)
-    lax.fori_loop(4, 8, forward, 0)
-    gathers[1].arrive_pair()
-    unfold(r.tiles, 3, 1, r.w_out)
-    unfold(r.tiles, 4, 4, r.w_up)
-    unfold_plain(r.tiles, 8, 4, r.w_down)
+
+        @pl.when(n == 6)
+        def _():
+            gathers[1].arrive(2)
+
+    loop(8, forward)
+    gathers[1].arrive_pair(0)
+    unfold(r, 3, r.w_out)
+    loop(2, lambda i: second_norm(r, i))
+    unfold(r, 4, r.w_up)
+    unfold(r, 5, r.w_up)
+    for part in (1, 2):
+        gathers[1].arrive_pair(part)
+    unfold(r, 6, r.w_up)
+    unfold(r, 7, r.w_up)
+    unfold_plain(r, r.w_down)
     gathers[0].settle()
     gathers[1].settle()
     tiny.settle()
-    lax.fori_loop(0, 2, lambda i, n: (second_norm(r, i), n)[1], 0)
-    load_y.wait()
-    lax.fori_loop(0, 4, lambda j, n: (feed_forward(r, j), n)[1], 0)
-    fold(r.g_up, r.tiles, 4, 4)
+    loads[9].wait()
+
+    def middle(j):
+        feed_forward(r, j)
+        pairs.tile(4 + j).start()
+        pairs.down(j).start()
+
+        @pl.when(j > 0)
+        def _():
+            pairs.add_tile(3 + j)
+            pairs.add_down(j - 1)
+
+    loop(4, middle)
+    second_norm_back(r, 0)
+    pairs.add_tile(7)
+    pairs.add_down(3)
     for part in (1, 2):
-        scatters[1].start_pair(part)
-    lax.fori_loop(0, 2, lambda i, n: (second_norm_back(r, i), n)[1], 0)
-    store_out.start()
+        scatters[1].start(part, 0)
+    second_norm_back(r, 1)
     out_gradient(r)
-    fold(r.g_out, r.tiles, 3, 1)
-    scatters[1].start_pair(0)
-    for part in (1, 2):
-        scatters[1].add_pair(part)
-        scatters[1].start(part, 0)
-
-    def backward(n, carry):
-        attend_back(r, lax.div(n, 4), lax.rem(n, 4))
+    pairs.tile(3).start()
+
+    def backward(n):
+        attend_back(r, lax.rem(n, 2), lax.div(n, 2))
 
         @pl.when(n == 0)
         def _():
-            scatters[1].add_pair(0)
+            pairs.add_tile(3)
             scatters[1].start(0, 0)
+
+        @pl.when(n == 3)
+        def _():
+            in_gradient(r, 0)
+            pairs.tile(0).start()
 
         @pl.when(n == 4)
         def _():
-            for part in (1, 2, 0):
+            pairs.add_tile(0)
+            scatters[0].start(0, 0)
+
+        @pl.when(n == 5)
+        def _():
+            in_gradient(r, 1)
+            pairs.tile(1).start()
+            for part in (1, 2):
                 scatters[1].add(part, 0)
                 scatters[1].start(part, 1)
 
         @pl.when(n == 6)
         def _():
-            for part in (1, 2, 0):
-                scatters[1].add(part, 1)
-                scatters[1].start(part, 2)
-
-        return carry
-
-    lax.fori_loop(0, 8, backward, 0)
-    in_gradient(r)
-    fold(r.g_qkv, r.tiles, 0, 3)
-    for part in range(3):
-        scatters[0].start_pair(part)
-    for part in range(3):
-        scatters[1].add(part, 2, r.total)
-    lax.fori_loop(0, 2, lambda i, n: (first_norm_back(r, i), n)[1], 0)
+            pairs.add_tile(1)
+            scatters[0].start(1, 0)
+            scatters[1].add(0, 0)
+            scatters[1].start(0, 1)
+            scatters[0].add(0, 0)
+            scatters[0].start(0, 1)
+
+    loop(8, backward)
+    in_gradient(r, 2)
+    pairs.tile(2).start()
+    for part in (1, 2):
+        scatters[1].add(part, 1)
+        scatters[1].start(part, 2)
+    first_norm_back(r, 0)
+    pairs.add_tile(2)
+    scatters[0].start(2, 0)
+    first_norm_back(r, 1)
     tiny_sum.pair_copy().start()
     store_glat.start()
-    for part in range(3):
-        scatters[0].add_pair(part)
-        scatters[0].start(part, 0)
+    scatters[1].add(0, 1)
+    scatters[1].start(0, 2)
+    for part in (0, 1):
+        scatters[0].add(part, 1 - part)
+        scatters[0].start(part, 2 - part)
     tiny_sum.add_pair()
     tiny_sum.start(0)
-    for stage in range(3):
-        for part in range(3):
-            scatters[0].add(part, stage, r.total)
-            if stage < 2:
-                scatters[0].start(part, stage + 1)
-        tiny_sum.add(stage)
-        if stage < 2:
-            tiny_sum.start(stage + 1)
-    r.s_total[...] = r.s_held[6]
+    result_of(r, 0)
+    scatters[0].add(2, 0)
+    scatters[0].start(2, 1)
+    result_of(r, 1)
+    store_out.start()
+    tiny_sum.add(0)
+    tiny_sum.start(1)
+    scatters[0].add(2, 1)
+    scatters[0].start(2, 2)
+    scatters[0].add(1, 1)
+    scatters[0].start(1, 2)
+    for part in (1, 2, 0):
+        scatters[1].add(part, 2, r.total)
+    tiny_sum.add(1)
+    tiny_sum.start(2)
+    for part in range(3):
+        scatters[0].add(part, 2, r.total)
     scatters[0].settle()
     scatters[1].settle()
-    tiny_sum.settle()
+    pairs.settle()
     store_out.wait()
     store_glat.wait()
-
-
-def whole(task_ids, counts, latents, cotangent, own, small):
+    tiny_sum.add(2)
+    r.s_total[...] = r.s_held[6]
+    tiny_sum.settle()
+
+
+def finish(*refs):
+    out_in, glat_in, total, small, out, glat, *rest = refs
+    table, norms, w_in, w_out, biases, w_up, up_bias, w_down, held, sems = rest
+    reads, writes = [], []
+    for n, (source, target) in enumerate(((out_in, out), (glat_in, glat))):
+        for i in range(2):
+            slot = 2 * n + i
+            reads.append(pltpu.make_async_copy(source.at[i], held.at[slot], sems.at[0, slot]))
+            writes.append(pltpu.make_async_copy(held.at[slot], target.at[i], sems.at[1, slot]))
+    for read in reads:
+        read.start()
+    for t, blocks in enumerate(COLUMNS):
+        to = (w_in, w_out, w_up)[0 if t < 3 else 1 if t == 3 else 2]
+        for q, ct in enumerate(blocks):
+            to[:, ct * 128 : (ct + 1) * 128] = total[t, 4 * q : 4 * q + 4]
+    for t in range(4):
+        w_down[:, t * 128 : (t + 1) * 128] = total[8 + t]
+    offset, bias_row, bias_offset = small_place(my_position())
+    block = pltpu.roll(small[...], lax.rem(128 - offset, 128), 1)
+    table[...] = block[0:18, 0:4]
+    norms[...] = block[18:22, 0:4]
+    biases[...] = block[22:24, 0:4]
+    row = lax.broadcasted_iota(jnp.int32, (32, 1), 0)
+    bias = jnp.sum(jnp.where(row == bias_row, small[...], 0.0), axis=0, keepdims=True)
+    bias = pltpu.roll(jnp.broadcast_to(bias, (8, 128)), lax.rem(128 - bias_offset, 128), 1)
+    up_bias[...] = bias[0:1, 0:16]
+    for read, write in zip(reads, writes, strict=True):
+        read.wait()
+        write.start()
+    for write in writes:
+        write.wait()
+
+
+def whole(task_ids, counts, latents, cotangent, *raw):
     vmem = pl.BlockSpec(memory_space=pltpu.VMEM)
     smem = pl.BlockSpec(memory_space=pltpu.SMEM)
     hbm = pl.BlockSpec(memory_space=pl.ANY)
     array = jax.ShapeDtypeStruct(latents.shape, BF16)
-    return pl.pallas_call(
+    found = pl.pallas_call(
         kernel,
         out_shape=[
             array,
@@ -774,14 +864,22 @@
             jax.ShapeDtypeStruct((TILES, 16, 128), F32),
             jax.ShapeDtypeStruct((32, 128), F32),
         ],
-        in_specs=[smem, smem, hbm, hbm, vmem, vmem],
+        in_specs=[smem, smem] + [hbm] * (2 + len(RAW)),
         out_specs=[hbm, hbm, vmem, vmem],
         scratch_shapes=[pltpu.VMEM(shape, dtype) for shape, dtype in SCRATCH.values()]
         + [pltpu.SemaphoreType.DMA(shape) for shape in SEMAPHORES.values()],
         compiler_params=pltpu.CompilerParams(
             collective_id=0, has_side_effects=True, vmem_limit_bytes=60 * 2**20
         ),
-    )(task_ids, counts, latents, cotangent, own, small)
+    )(task_ids, counts, latents, cotangent, *raw)
+    shapes = ((18, 4), (4, 4), (4, 1536), (4, 512), (2, 4), (4, 2048), (1, 16), (16, 512))
+    return pl.pallas_call(
+        finish,
+        out_shape=[array, array] + [jax.ShapeDtypeStruct(shape, F32) for shape in shapes],
+        in_specs=[hbm, hbm, vmem, vmem],
+        out_specs=[hbm, hbm] + [vmem] * 8,
+        scratch_shapes=[pltpu.VMEM((4, 512, 512), BF16), pltpu.SemaphoreType.DMA((2, 4))],
+    )(*found)
 
 
 def body(
@@ -798,12 +896,10 @@
     mlp_in_bias,
     mlp_out,
 ):
-    own = shard_tiles(attn_in, attn_out, mlp_in, mlp_out)
-    small = shard_small(task_embed, norms, out_biases, mlp_in_bias)
-    result, grad_lat, total, s_total = whole(task_ids, slot_counts, latents, cotangent, own, small)
-    s_qkv, s_out, s_up, s_down = own_weights(total)
-    s_table, s_norms, s_biases, s_bias = own_small(s_total)
-    return (result, grad_lat, s_table, s_norms, s_qkv, s_out, s_biases, s_up, s_bias, s_down)
+    raw = (attn_in, attn_out, mlp_in, mlp_out, task_embed, norms, out_biases, mlp_in_bias.reshape(1, 16))
+    found = list(whole(task_ids, slot_counts, latents, cotangent, *raw))
+    found[8] = found[8].reshape(16)
+    return tuple(found)
 
 
 def solution(mesh):

time: 135 us -> 107 us (0.79)
  local copies, waits for them, and re-layouts: 17.9 us -> 2.73 us
  Pallas kernels: 115 us -> 103 us
    pallas_call x1, Pallas kernels: 115 us -> 99.4 us  [whole(): pl.pallas_call(kernel, out_shape=[array, array, jax.ShapeDtypeStruct((TIL...]
    unnamed x25 -> x6, local copies, waits for them, and re-layouts: 8.72 us -> 2.73 us
    slice x5 -> x0, local copies, waits for them, and re-layouts: 5.42 us -> none  [the longest x3 3.39 us: own_small(): return (columns[0:18], columns[18:22], columns[22:24], bias)]
    pallas_call x0 -> x1, Pallas kernels: none -> 3.99 us  [whole(): pl.pallas_call(finish, out_shape=[array, array] + [jax.ShapeDtypeStruct(s...]
    reshape x7 -> x0, local copies, waits for them, and re-layouts: 1.95 us -> none  [the longest x3 1.29 us: quarters(): t.reshape(count, 4, 4, 128).transpose(2, 1, 0, 3)]
where the time goes in v1:
time: 107 us
  Pallas kernels  103 us (96%)
  local copies, waits for them, and re-layouts  2.73 us (3%)
    pallas_call x1, Pallas kernels, whole(): pl.pallas_call(kernel, out_shape=[array, array, jax.ShapeDtypeStruct((TIL...  99.4 us
    pallas_call x1, Pallas kernels, whole(): pl.pallas_call(finish, out_shape=[array, array] + [jax.ShapeDtypeStruct(s...  3.99 us
    unnamed x6, local copies, waits for them, and re-layouts  2.73 us

profile of v1, /device:TPU:0, one launch (start us, length us, event | category | flops | bytes accessed | tf_op | source)
XLA Modules:
  0.0 106.7 jit_solution(7447960261917269816)
XLA Ops:
  0.6 0.0 copy-start.1
  0.7 0.7 copy-done.1
  1.3 0.7 copy.22.refs_8_
  2.0 99.4 %shard_map.195 = (bf16[2,512,512]{2,1,0:T(8,128)(2,1)}, bf16[2,512,512]{2,1,0:T(8,128)(2,1)}, f32[12,16,128]{2,1,0:T(8,128)}, f32[32,128]{1,0:T(8,128)}) custom-call(s32[2]{0:T(128)} %refs_0_.1, s32[2]{0:T(128)} %refs_1_.1, bf16[2,512,512]{2,1,0:T(8,128)(2,1)} %refs_2_.1, bf16[2,512,512]{2,1,0:T(8,128)(2,1)} %refs_3_.1, bf16[4,1536]{1,0:T(4,128)(2,1)} %refs_4_.1, ...), custom_call_target="tpu_custom_call" | custom-call | tf_op jit(solution)/shard_map/pallas_call | solution.py:859
  101.4 4.0 %shard_map.196 = (bf16[2,512,512]{2,1,0:T(8,128)(2,1)}, bf16[2,512,512]{2,1,0:T(8,128)(2,1)}, f32[18,4]{1,0:T(8,128)}, f32[4,4]{1,0:T(4,128)}, f32[4,1536]{1,0:T...) custom-call(bf16[2,512,512]{2,1,0:T(8,128)(2,1)} %get-tuple-element., ...), custom_call_target="tpu_custom_call" | custom-call | tf_op jit(solution)/shard_map/pallas_call | solution.py:876
  105.4 0.0 copy-start
  105.4 0.7 copy-done
  106.1 0.7 copy.23
Async XLA Ops:
  0.6 0.7 copy-start.1
  105.4 0.7 copy-start
